TPU v7x, 32 devices: a whole 2x2x4 slice. The times are simulated.
32 devices in a mesh: groups: 2 (over x), col: 16 (over z, y, core).
Axes of the slice: x: 2, y: 2, z: 4, core: 2. Of those that a mesh axis runs over, the one named last changes fastest.
Arguments:
- coords: bfloat16 [3, 131072], P(None, ('groups', 'col')), parts along dimension 1, may hold values from 0 to 8
- probes: bfloat16 [64, 131072], P(None, ('groups', 'col')), parts along dimension 1, may hold values from -6 to 6
- order: int32 [131072], P(('groups', 'col')), parts along dimension 0, may hold values from 0 to 65535, as said below
- near_list: int32 [512, 27], P(('groups', 'col')), parts along dimension 0, may hold values from -16 to 271, as said below
- near_count: int32 [512], P(('groups', 'col')), parts along dimension 0, may hold values from 1 to 27
- leaf_basis: bfloat16 [512, 64, 256], P(('groups', 'col')), parts along dimension 0, may hold values from -0.375 to 0.375
- transfer_low: bfloat16 [512, 64, 64], P(('groups', 'col')), parts along dimension 0, may hold values from -0.5 to 0.5
- transfer_top: bfloat16 [256, 64, 64], P(('groups', 'col')), parts along dimension 0, may hold values from -0.5 to 0.5
- coupling_leaf: bfloat16 [512, 16, 64, 64], P(('groups', 'col')), parts along dimension 0, may hold values from -0.1875 to 0.1875
- coupling_mid: bfloat16 [256, 16, 64, 64], P(('groups', 'col')), parts along dimension 0, may hold values from -0.1875 to 0.1875
- coupling_top: bfloat16 [128, 16, 64, 64], P(('groups', 'col')), parts along dimension 0, may hold values from -0.1875 to 0.1875
- far_leaf: int32 [512, 16], P(('groups', 'col')), parts along dimension 0, may hold values from -16 to 271, as said below
- far_mid: int32 [256, 16], P(('groups', 'col')), parts along dimension 0, may hold values from -8 to 135, as said below
- far_top: int32 [128, 16], P(('groups', 'col')), parts along dimension 0, may hold values from 0 to 63, as said below
Outputs:
- kernel_product: float32 [64, 131072], P(None, ('groups', 'col')), parts along dimension 1
There are 2 independent parts, one for each index of `groups`. A program takes and returns all parts, laid end to end along the dimension named above; each array names one. Nothing has to cross between parts.
Inputs may be any that keep to these rules, and one draw needn't show every extreme that they name: `order`: each aligned block of 4096 entries is a permutation of that block's own positions. `near_list`: slot 0 of leaf i names i itself; every entry lies within 16 of its leaf's index. `far_leaf`: every entry lies within 16 of its cluster's index. `far_mid`: every entry lies within 8 of its cluster's index. `far_top`: in each aligned block of 4 rows, the entries name at most one cluster of each aligned range of 4 top-level clusters.
All inputs are finite; a program needn't handle non-finite values.
Results may differ from a plain program's by a relative error of at most 0.0034.
The roundings to bfloat16 on the way count: a program that leaves them out, or rounds other values in their place, can miss the bound.
Values may be sent and summed in bfloat16 or wider, within the bound.
A program may use at most 128 MiB of HBM per device.

v0:
```python
import math

import jax
import jax.numpy as jnp
from jax import lax
from jax.sharding import PartitionSpec as P

LEAF = 256
NEAR = 27


AMPLITUDE = 0.125
LENGTH_SCALE = 1.0


def padded(cells, sides, width):
    for axis, dim in sides:
        count = lax.axis_size(axis)
        ends = count - 1
        head = lax.slice_in_dim(cells, 0, width, axis=dim)
        tail = lax.slice_in_dim(cells, cells.shape[dim] - width, cells.shape[dim], axis=dim)
        cells = jnp.concatenate(
            [
                lax.ppermute(tail, axis, [(i, (i + 1) % count) for i in range(ends)]),
                cells,
                lax.ppermute(head, axis, [((i + 1) % count, i) for i in range(ends)]),
            ],
            axis=dim,
        )
    return cells


def kernel_rows(target, source):
    running = jnp.zeros((source.shape[0], target.shape[1], source.shape[2]), jnp.float32)
    for axis_id in range(3):
        spacing = (
            target[axis_id].astype(jnp.float32)[None, :, None]
            - source[:, axis_id].astype(jnp.float32)[:, None, :]
        )
        running = running + spacing * spacing
    return (AMPLITUDE * jnp.exp(-jnp.sqrt(running) / LENGTH_SCALE)).astype(jnp.bfloat16)


def apply_coupling(rows, positions, coupling):
    sources = jnp.take(rows, positions, axis=0)
    sources = sources.reshape(positions.shape + (coupling.shape[2], coupling.shape[3]))
    return jnp.einsum("nfpr,nfrs->nps", sources, coupling, preferred_element_type=jnp.float32)


def lift(child, transfer):
    paired_child = child.reshape((child.shape[0] // 2, 2) + child.shape[1:])
    paired_transfer = transfer.reshape((child.shape[0] // 2, 2) + transfer.shape[1:])
    return jnp.einsum(
        "mcpr,mcrs->mps", paired_child, paired_transfer, preferred_element_type=jnp.float32
    ).astype(jnp.bfloat16)


def lower(parent_rounded, transfer, couple_child):
    paired = transfer.reshape((parent_rounded.shape[0], 2) + transfer.shape[1:])
    moved = jnp.einsum("mpr,mcqr->mcpq", parent_rounded, paired, preferred_element_type=jnp.float32)
    return (couple_child + moved.reshape(couple_child.shape)).astype(jnp.bfloat16)


def per_device(
    coords,
    probes,
    order,
    near_list,
    near_count,
    leaf_basis,
    transfer_low,
    transfer_top,
    coupling_leaf,
    coupling_mid,
    coupling_top,
    far_leaf,
    far_mid,
    far_top,
):
    probe_rows = probes.shape[0]
    point_count = probes.shape[1]
    leaves = point_count // LEAF
    rank_width = leaf_basis.shape[1]
    device_index = lax.axis_index("col")
    local_order = order - device_index * point_count
    block_width = math.gcd(point_count, 512)
    block_total = point_count // block_width
    point_ids = jnp.arange(point_count, dtype=jnp.int32)
    stacked = jnp.concatenate([coords, probes], axis=0)
    order_blocks = local_order.reshape(block_total, block_width)

    def gather_block(wanted):
        selector = (point_ids[:, None] == wanted[None, :]).astype(jnp.bfloat16)
        return jnp.dot(stacked, selector, preferred_element_type=jnp.float32).astype(jnp.bfloat16)

    tree_blocks = lax.map(gather_block, order_blocks)
    tree_rows = jnp.moveaxis(tree_blocks, 0, 1).reshape(3 + probe_rows, point_count)
    leaf_major = jnp.moveaxis(tree_rows.reshape(3 + probe_rows, leaves, LEAF), 1, 0)
    extended = padded(leaf_major, (("col", 0),), leaves)
    leaf_offset = device_index * leaves - leaves

    def near_leaf(inputs):
        neighbors, live_count, target = inputs
        sources = jnp.take(extended, neighbors - leaf_offset, axis=0)
        kernel_block = kernel_rows(target, sources[:, :3])
        live_mask = (jnp.arange(NEAR, dtype=jnp.int32) < live_count).astype(jnp.bfloat16)
        masked_values = sources[:, 3:] * live_mask[:, None, None]
        return jnp.einsum(
            "nts,nps->pt", kernel_block, masked_values, preferred_element_type=jnp.float32
        )

    near_blocks = lax.map(near_leaf, (near_list, near_count, leaf_major[:, :3]))
    near_field = jnp.moveaxis(near_blocks, 0, 1).reshape(probe_rows, point_count)
    probe_blocks = tree_rows[3:].reshape(probe_rows, leaves, LEAF)
    coeff_leaf = jnp.einsum(
        "plq,lrq->lpr", probe_blocks, leaf_basis, preferred_element_type=jnp.float32
    ).astype(jnp.bfloat16)
    coeff_mid = lift(coeff_leaf, transfer_low)
    coeff_top = lift(coeff_mid, transfer_top)
    flat_width = probe_rows * rank_width
    around_leaf = padded(coeff_leaf.reshape(leaves, flat_width), (("col", 0),), leaves)
    couple_leaf = apply_coupling(around_leaf, far_leaf - leaf_offset, coupling_leaf)
    mid_count = leaves // 2
    around_mid = padded(coeff_mid.reshape(mid_count, flat_width), (("col", 0),), mid_count)
    couple_mid = apply_coupling(
        around_mid, far_mid - (device_index * mid_count - mid_count), coupling_mid
    )
    top_count = leaves // 4
    top_flat = coeff_top.reshape(top_count, flat_width)
    gathered = lax.all_gather(top_flat, "col", axis=0, tiled=True)
    couple_top = apply_coupling(gathered, far_top, coupling_top)
    top_rounded = couple_top.astype(jnp.bfloat16)
    down_mid = lower(top_rounded, transfer_top, couple_mid)
    down_leaf = lower(down_mid, transfer_low, couple_leaf)
    far_field = jnp.einsum(
        "lpr,lrq->plq", down_leaf, leaf_basis, preferred_element_type=jnp.float32
    ).reshape(probe_rows, point_count)
    combined = near_field + far_field

    def place_block(first_column):
        columns = first_column + jnp.arange(block_width, dtype=jnp.int32)
        selector = (local_order[:, None] == columns[None, :]).astype(jnp.float32)
        return jnp.dot(
            combined, selector, precision=lax.Precision.HIGHEST, preferred_element_type=jnp.float32
        )

    placed = lax.map(place_block, jnp.arange(block_total, dtype=jnp.int32) * block_width)
    return jnp.moveaxis(placed, 0, 1).reshape(probe_rows, point_count)


def solution(mesh):
    return jax.shard_map(
        per_device,
        mesh=mesh,
        in_specs=(
            P(None, ("groups", "col")),
            P(None, ("groups", "col")),
            P(("groups", "col")),
            P(("groups", "col"), None),
            P(("groups", "col")),
            P(("groups", "col"), None, None),
            P(("groups", "col"), None, None),
            P(("groups", "col"), None, None),
            P(("groups", "col"), None, None, None),
            P(("groups", "col"), None, None, None),
            P(("groups", "col"), None, None, None),
            P(("groups", "col"), None),
            P(("groups", "col"), None),
            P(("groups", "col"), None),
        ),
        out_specs=P(None, ("groups", "col")),
        check_vma=False,
    )
```

profile of v0, /device:TPU:5, one launch (start us, length us, event | category | flops | bytes accessed | tf_op | source)
XLA Modules:
  0.0 355.1 jit_solution(16515465188112999802)
XLA Ops:
  2.9 20.5 %while.33 = (s32[]{:T(128)}, bf16[8,67,512]{2,1,0:T(8,128)(2,1)S(1)}, s32[8,512]{1,0:T(8,128)S(1)}, bf16[67,4096]{1,0:T(8,128)(2,1)}, s32[]{:T(128)}) while((s32[]{:T(128)}, bf16[8,67,512]{2,1,0:T(8,128)(2,1)S(1)}, s32[8,512]{1,0:T(8,128)S(1)}, bf16[67,4096]{1,0:T(8,128)(2,1)}, s32[]{:T(128)}) %tuple.62), condition=%wide.region_1.2_spmd.clone, body=%wide.region_0.1_spmd.clone.sunk | while | flops 283149824 | bytes 628805 | solution.py:96
  34.3 4.5 %collective-permute-start.2 = (bf16[16,4096]{1,0:T(8,128)(2,1)S(1)}, bf16[16,4096]{1,0:T(8,128)(2,1)}, u32[]{:S(2)}, u32[]{:S(2)}) collective-permute-start(bf16[16,4096]{1,0:T(8,128)(2,1)S(1)} %reshape.136), channel_id=1, source_target_pairs={{0,1},{1,2},{2,3},{3,4},{4,5},{5,6},{6,7},{7,8},{8,9},{9,10},{10,1... | collective-permute-start | bytes 393224 | tf_op jit(solution)/shard_map/ppermute | solution.py:24
  41.9 4.5 %collective-permute-start = (bf16[16,67,256]{2,0,1:T(8,128)(2,1)}, bf16[16,67,256]{2,0,1:T(8,128)(2,1)}, u32[]{:S(2)}, u32[]{:S(2)}) collective-permute-start(bf16[16,67,256]{2,0,1:T(8,128)(2,1)} %bitcast.13), channel_id=1, source_target_pairs={{0,1},{1,2},{2,3},{3,4},{4,5},{5,6},{6,7},{7,8},{8,9},{9,10},{10,1... | collective-permute-start | bytes 1646600 | tf_op jit(solution)/shard_map/ppermute | solution.py:24
  50.3 18.8 %all-gather = bf16[16,4,4096]{2,1,0:T(4,128)(2,1)S(1)} all-gather(bf16[1,4,4096]{2,1,0:T(4,128)(2,1)S(1)} %reshape.193), channel_id=1, replica_groups=mesh['groups'=2,'col'=16] {'col'}, dimensions={0}, use_global_device_ids=true | all-gather | bytes 557056 | tf_op jit(solution)/shard_map/all_gather | solution.py:130
  89.9 6.9 %gather.23 = bf16[16,16,64,64]{3,2,1,0:T(8,128)(2,1)} reshape(bf16[256,4096]{1,0:T(8,128)(2,1)} %gather_fusion.1) | data formatting | bytes 4194304 | tf_op jit(solution)/shard_map/jit(_take)/gather | solution.py:45
  96.9 6.2 %fusion.44 = f32[16,64,256]{2,1,0:T(8,128)} fusion(bf16[16,64,256]{2,1,0:T(8,128)(2,1)S(1)} %copy-done.3, f32[16,64,64]{2,1,0:T(8,128)S(1)} %bitcast.166, bf16[16,16,64,64]{3,2,1,0:T(8,128)(2,1)} %param.28, bf16[16,16,64,64]{3,2,1,0:T(8,128)(2,1)} %gather.23, pred[16,16]{1,0:T(8,128)(4,1)S(1)} %get-tuple-element.155), kind=kOutput, calls=%fused_computation.59 | convolution fusion | flops 168951808 | bytes 6029568 | tf_op jit(solution)/shard_map/lpr,lrq->plq/dot_general | solution.py:135
  106.4 200.5 %while.31 = (s32[]{:T(128)}, f32[16,64,256]{2,1,0:T(8,128)}, s32[16,27]{1,0:T(8,128)}, s32[]{:T(128)}, bf16[48,67,256]{2,1,0:T(8,128)(2,1)}, /*index=5*/s32[16]{...) while((s32[]{:T(128)}, f32[16,64,256]{2,1,0:T(8,128)}, ...), condition=%wide.region_3.4_spmd, body=%wide.region_2.3_spmd.sunk | while | flops 246884960 | bytes 8746379 | solution.py:112
  112.4 6.5 %fusion.104 = f32[16,64,256]{2,1,0:T(8,128)} fusion(f32[16,64,256]{2,1,0:T(8,128)} %get-tuple-element.309, s32[]{:T(128)} %get-tuple-element.308, f32[27,256]{1,0:T(8,128)S(1)} %get-tuple-element.267, f32[256]{0:T(256)S(1)} %bitcast.165, f32[27,256]{1,0:T(8,128)S(1)} %get-tuple-element.269, f32[256]{0:T(256)S(1)} %bitcast.164, ...), kind=kOutput, calls=%fused_computation.15.clone.1 | convolution fusion | flops 246398976 | bytes 1036854 | tf_op jit(solution)/shard_map/while/body/eval_jaxpr/nts,nps->pt/dot_general | solution.py:108
  125.0 6.5 %fusion.104 = f32[16,64,256]{2,1,0:T(8,128)} fusion(f32[16,64,256]{2,1,0:T(8,128)} %get-tuple-element.309, s32[]{:T(128)} %get-tuple-element.308, f32[27,256]{1,0:T(8,128)S(1)} %get-tuple-element.267, f32[256]{0:T(256)S(1)} %bitcast.165, f32[27,256]{1,0:T(8,128)S(1)} %get-tuple-element.269, f32[256]{0:T(256)S(1)} %bitcast.164, ...), kind=kOutput, calls=%fused_computation.15.clone.1 | convolution fusion | flops 246398976 | bytes 1036854 | tf_op jit(solution)/shard_map/while/body/eval_jaxpr/nts,nps->pt/dot_general | solution.py:108
  137.5 6.5 %fusion.104 = f32[16,64,256]{2,1,0:T(8,128)} fusion(f32[16,64,256]{2,1,0:T(8,128)} %get-tuple-element.309, s32[]{:T(128)} %get-tuple-element.308, f32[27,256]{1,0:T(8,128)S(1)} %get-tuple-element.267, f32[256]{0:T(256)S(1)} %bitcast.165, f32[27,256]{1,0:T(8,128)S(1)} %get-tuple-element.269, f32[256]{0:T(256)S(1)} %bitcast.164, ...), kind=kOutput, calls=%fused_computation.15.clone.1 | convolution fusion | flops 246398976 | bytes 1036854 | tf_op jit(solution)/shard_map/while/body/eval_jaxpr/nts,nps->pt/dot_general | solution.py:108
  150.0 6.5 %fusion.104 = f32[16,64,256]{2,1,0:T(8,128)} fusion(f32[16,64,256]{2,1,0:T(8,128)} %get-tuple-element.309, s32[]{:T(128)} %get-tuple-element.308, f32[27,256]{1,0:T(8,128)S(1)} %get-tuple-element.267, f32[256]{0:T(256)S(1)} %bitcast.165, f32[27,256]{1,0:T(8,128)S(1)} %get-tuple-element.269, f32[256]{0:T(256)S(1)} %bitcast.164, ...), kind=kOutput, calls=%fused_computation.15.clone.1 | convolution fusion | flops 246398976 | bytes 1036854 | tf_op jit(solution)/shard_map/while/body/eval_jaxpr/nts,nps->pt/dot_general | solution.py:108
  162.6 6.5 %fusion.104 = f32[16,64,256]{2,1,0:T(8,128)} fusion(f32[16,64,256]{2,1,0:T(8,128)} %get-tuple-element.309, s32[]{:T(128)} %get-tuple-element.308, f32[27,256]{1,0:T(8,128)S(1)} %get-tuple-element.267, f32[256]{0:T(256)S(1)} %bitcast.165, f32[27,256]{1,0:T(8,128)S(1)} %get-tuple-element.269, f32[256]{0:T(256)S(1)} %bitcast.164, ...), kind=kOutput, calls=%fused_computation.15.clone.1 | convolution fusion | flops 246398976 | bytes 1036854 | tf_op jit(solution)/shard_map/while/body/eval_jaxpr/nts,nps->pt/dot_general | solution.py:108
  175.1 6.5 %fusion.104 = f32[16,64,256]{2,1,0:T(8,128)} fusion(f32[16,64,256]{2,1,0:T(8,128)} %get-tuple-element.309, s32[]{:T(128)} %get-tuple-element.308, f32[27,256]{1,0:T(8,128)S(1)} %get-tuple-element.267, f32[256]{0:T(256)S(1)} %bitcast.165, f32[27,256]{1,0:T(8,128)S(1)} %get-tuple-element.269, f32[256]{0:T(256)S(1)} %bitcast.164, ...), kind=kOutput, calls=%fused_computation.15.clone.1 | convolution fusion | flops 246398976 | bytes 1036854 | tf_op jit(solution)/shard_map/while/body/eval_jaxpr/nts,nps->pt/dot_general | solution.py:108
  187.6 6.5 %fusion.104 = f32[16,64,256]{2,1,0:T(8,128)} fusion(f32[16,64,256]{2,1,0:T(8,128)} %get-tuple-element.309, s32[]{:T(128)} %get-tuple-element.308, f32[27,256]{1,0:T(8,128)S(1)} %get-tuple-element.267, f32[256]{0:T(256)S(1)} %bitcast.165, f32[27,256]{1,0:T(8,128)S(1)} %get-tuple-element.269, f32[256]{0:T(256)S(1)} %bitcast.164, ...), kind=kOutput, calls=%fused_computation.15.clone.1 | convolution fusion | flops 246398976 | bytes 1036854 | tf_op jit(solution)/shard_map/while/body/eval_jaxpr/nts,nps->pt/dot_general | solution.py:108
  200.2 6.5 %fusion.104 = f32[16,64,256]{2,1,0:T(8,128)} fusion(f32[16,64,256]{2,1,0:T(8,128)} %get-tuple-element.309, s32[]{:T(128)} %get-tuple-element.308, f32[27,256]{1,0:T(8,128)S(1)} %get-tuple-element.267, f32[256]{0:T(256)S(1)} %bitcast.165, f32[27,256]{1,0:T(8,128)S(1)} %get-tuple-element.269, f32[256]{0:T(256)S(1)} %bitcast.164, ...), kind=kOutput, calls=%fused_computation.15.clone.1 | convolution fusion | flops 246398976 | bytes 1036854 | tf_op jit(solution)/shard_map/while/body/eval_jaxpr/nts,nps->pt/dot_general | solution.py:108
  212.7 6.5 %fusion.104 = f32[16,64,256]{2,1,0:T(8,128)} fusion(f32[16,64,256]{2,1,0:T(8,128)} %get-tuple-element.309, s32[]{:T(128)} %get-tuple-element.308, f32[27,256]{1,0:T(8,128)S(1)} %get-tuple-element.267, f32[256]{0:T(256)S(1)} %bitcast.165, f32[27,256]{1,0:T(8,128)S(1)} %get-tuple-element.269, f32[256]{0:T(256)S(1)} %bitcast.164, ...), kind=kOutput, calls=%fused_computation.15.clone.1 | convolution fusion | flops 246398976 | bytes 1036854 | tf_op jit(solution)/shard_map/while/body/eval_jaxpr/nts,nps->pt/dot_general | solution.py:108
  225.2 6.5 %fusion.104 = f32[16,64,256]{2,1,0:T(8,128)} fusion(f32[16,64,256]{2,1,0:T(8,128)} %get-tuple-element.309, s32[]{:T(128)} %get-tuple-element.308, f32[27,256]{1,0:T(8,128)S(1)} %get-tuple-element.267, f32[256]{0:T(256)S(1)} %bitcast.165, f32[27,256]{1,0:T(8,128)S(1)} %get-tuple-element.269, f32[256]{0:T(256)S(1)} %bitcast.164, ...), kind=kOutput, calls=%fused_computation.15.clone.1 | convolution fusion | flops 246398976 | bytes 1036854 | tf_op jit(solution)/shard_map/while/body/eval_jaxpr/nts,nps->pt/dot_general | solution.py:108
  237.8 6.5 %fusion.104 = f32[16,64,256]{2,1,0:T(8,128)} fusion(f32[16,64,256]{2,1,0:T(8,128)} %get-tuple-element.309, s32[]{:T(128)} %get-tuple-element.308, f32[27,256]{1,0:T(8,128)S(1)} %get-tuple-element.267, f32[256]{0:T(256)S(1)} %bitcast.165, f32[27,256]{1,0:T(8,128)S(1)} %get-tuple-element.269, f32[256]{0:T(256)S(1)} %bitcast.164, ...), kind=kOutput, calls=%fused_computation.15.clone.1 | convolution fusion | flops 246398976 | bytes 1036854 | tf_op jit(solution)/shard_map/while/body/eval_jaxpr/nts,nps->pt/dot_general | solution.py:108
  250.3 6.5 %fusion.104 = f32[16,64,256]{2,1,0:T(8,128)} fusion(f32[16,64,256]{2,1,0:T(8,128)} %get-tuple-element.309, s32[]{:T(128)} %get-tuple-element.308, f32[27,256]{1,0:T(8,128)S(1)} %get-tuple-element.267, f32[256]{0:T(256)S(1)} %bitcast.165, f32[27,256]{1,0:T(8,128)S(1)} %get-tuple-element.269, f32[256]{0:T(256)S(1)} %bitcast.164, ...), kind=kOutput, calls=%fused_computation.15.clone.1 | convolution fusion | flops 246398976 | bytes 1036854 | tf_op jit(solution)/shard_map/while/body/eval_jaxpr/nts,nps->pt/dot_general | solution.py:108
  262.8 6.5 %fusion.104 = f32[16,64,256]{2,1,0:T(8,128)} fusion(f32[16,64,256]{2,1,0:T(8,128)} %get-tuple-element.309, s32[]{:T(128)} %get-tuple-element.308, f32[27,256]{1,0:T(8,128)S(1)} %get-tuple-element.267, f32[256]{0:T(256)S(1)} %bitcast.165, f32[27,256]{1,0:T(8,128)S(1)} %get-tuple-element.269, f32[256]{0:T(256)S(1)} %bitcast.164, ...), kind=kOutput, calls=%fused_computation.15.clone.1 | convolution fusion | flops 246398976 | bytes 1036854 | tf_op jit(solution)/shard_map/while/body/eval_jaxpr/nts,nps->pt/dot_general | solution.py:108
  275.4 6.5 %fusion.104 = f32[16,64,256]{2,1,0:T(8,128)} fusion(f32[16,64,256]{2,1,0:T(8,128)} %get-tuple-element.309, s32[]{:T(128)} %get-tuple-element.308, f32[27,256]{1,0:T(8,128)S(1)} %get-tuple-element.267, f32[256]{0:T(256)S(1)} %bitcast.165, f32[27,256]{1,0:T(8,128)S(1)} %get-tuple-element.269, f32[256]{0:T(256)S(1)} %bitcast.164, ...), kind=kOutput, calls=%fused_computation.15.clone.1 | convolution fusion | flops 246398976 | bytes 1036854 | tf_op jit(solution)/shard_map/while/body/eval_jaxpr/nts,nps->pt/dot_general | solution.py:108
  287.9 6.5 %fusion.104 = f32[16,64,256]{2,1,0:T(8,128)} fusion(f32[16,64,256]{2,1,0:T(8,128)} %get-tuple-element.309, s32[]{:T(128)} %get-tuple-element.308, f32[27,256]{1,0:T(8,128)S(1)} %get-tuple-element.267, f32[256]{0:T(256)S(1)} %bitcast.165, f32[27,256]{1,0:T(8,128)S(1)} %get-tuple-element.269, f32[256]{0:T(256)S(1)} %bitcast.164, ...), kind=kOutput, calls=%fused_computation.15.clone.1 | convolution fusion | flops 246398976 | bytes 1036854 | tf_op jit(solution)/shard_map/while/body/eval_jaxpr/nts,nps->pt/dot_general | solution.py:108
  300.4 6.5 %fusion.104 = f32[16,64,256]{2,1,0:T(8,128)} fusion(f32[16,64,256]{2,1,0:T(8,128)} %get-tuple-element.309, s32[]{:T(128)} %get-tuple-element.308, f32[27,256]{1,0:T(8,128)S(1)} %get-tuple-element.267, f32[256]{0:T(256)S(1)} %bitcast.165, f32[27,256]{1,0:T(8,128)S(1)} %get-tuple-element.269, f32[256]{0:T(256)S(1)} %bitcast.164, ...), kind=kOutput, calls=%fused_computation.15.clone.1 | convolution fusion | flops 246398976 | bytes 1036854 | tf_op jit(solution)/shard_map/while/body/eval_jaxpr/nts,nps->pt/dot_general | solution.py:108
  309.9 44.1 %while.32 = (s32[]{:T(128)}, f32[8,64,512]{2,1,0:T(8,128)S(1)}, s32[4096]{0:T(1024)S(1)}, s32[8]{0:T(128)S(1)}, f32[64,4096]{1,0:T(8,128)}, /*index=5*/s32[]{:T(128)}) while((s32[]{:T(128)}, f32[8,64,512]{2,1,0:T(8,128)S(1)}, s32[4096]{0:T(1024)S(1)}, s32[8]{0:T(128)S(1)}, f32[64,4096]{1,0:T(8,128)}, /*index=5*/s32[]{:T(128)}) %tuple.73), condition=%wide.region_5.6_spmd, body=%wide.region_4.5_spmd.sunk | while | flops 1612710400 | bytes 1200217 | solution.py:147
  (329 shorter events, 207.8 us)
Async XLA Ops:
  0.0 82.9 %copy-start = (bf16[8,16,64,64]{3,2,1,0:T(8,128)(2,1)S(1)}, bf16[8,16,64,64]{3,2,1,0:T(8,128)(2,1)}, u32[]{:S(2)}) copy-start(bf16[8,16,64,64]{3,2,1,0:T(8,128)(2,1)} %param.29) | copy-start | bytes 3145732
  0.9 2.0 copy-start.5
  23.6 22.9 %copy-start.9 = (s32[4,16]{1,0:T(4,128)S(1)}, s32[4,16]{1,0:T(4,128)}, u32[]{:S(2)}) copy-start(s32[4,16]{1,0:T(4,128)} %param.33) | copy-start | bytes 772
  23.6 24.2 %copy-start.10 = (s32[8,16]{1,0:T(8,128)S(1)}, s32[8,16]{1,0:T(8,128)}, u32[]{:S(2)}) copy-start(s32[8,16]{1,0:T(8,128)} %param.32) | copy-start | bytes 1540
  28.4 46.9 %collective-permute-start.4 = (bf16[8,4096]{1,0:T(8,128)(2,1)}, bf16[8,4096]{1,0:T(8,128)(2,1)}, u32[]{:S(2)}, u32[]{:S(2)}) collective-permute-start(bf16[8,4096]{1,0:T(8,128)(2,1)} %reshape.139), channel_id=1, source_target_pairs={{0,1},{1,2},{2,3},{3,4},{4,5},{5,6},{6,7},{7,8},{8,9},{9,10},{10,1... | collective-permute-start | bytes 196616 | tf_op jit(solution)/shard_map/ppermute | solution.py:24
  32.1 45.3 %collective-permute-start.5 = (bf16[8,4096]{1,0:T(8,128)(2,1)}, bf16[8,4096]{1,0:T(8,128)(2,1)}, u32[]{:S(2)}, u32[]{:S(2)}) collective-permute-start(bf16[8,4096]{1,0:T(8,128)(2,1)} %reshape.139), channel_id=1, source_target_pairs={{1,0},{2,1},{3,2},{4,3},{5,4},{6,5},{7,6},{8,7},{9,8},{10,9},{11,1... | collective-permute-start | bytes 196616 | tf_op jit(solution)/shard_map/ppermute | solution.py:26
  34.3 51.4 %collective-permute-start.2 = (bf16[16,4096]{1,0:T(8,128)(2,1)S(1)}, bf16[16,4096]{1,0:T(8,128)(2,1)}, u32[]{:S(2)}, u32[]{:S(2)}) collective-permute-start(bf16[16,4096]{1,0:T(8,128)(2,1)S(1)} %reshape.136), channel_id=1, source_target_pairs={{0,1},{1,2},{2,3},{3,4},{4,5},{5,6},{6,7},{7,8},{8,9},{9,10},{10,1... | collective-permute-start | bytes 393224 | tf_op jit(solution)/shard_map/ppermute | solution.py:24
  38.8 46.9 %collective-permute-start.3 = (bf16[16,4096]{1,0:T(8,128)(2,1)S(1)}, bf16[16,4096]{1,0:T(8,128)(2,1)}, u32[]{:S(2)}, u32[]{:S(2)}) collective-permute-start(bf16[16,4096]{1,0:T(8,128)(2,1)S(1)} %reshape.136), channel_id=1, source_target_pairs={{1,0},{2,1},{3,2},{4,3},{5,4},{6,5},{7,6},{8,7},{9,8},{10,9},{11,1... | collective-permute-start | bytes 393224 | tf_op jit(solution)/shard_map/ppermute | solution.py:26
  41.9 61.1 %collective-permute-start = (bf16[16,67,256]{2,0,1:T(8,128)(2,1)}, bf16[16,67,256]{2,0,1:T(8,128)(2,1)}, u32[]{:S(2)}, u32[]{:S(2)}) collective-permute-start(bf16[16,67,256]{2,0,1:T(8,128)(2,1)} %bitcast.13), channel_id=1, source_target_pairs={{0,1},{1,2},{2,3},{3,4},{4,5},{5,6},{6,7},{7,8},{8,9},{9,10},{10,1... | collective-permute-start | bytes 1646600 | tf_op jit(solution)/shard_map/ppermute | solution.py:24
  69.0 3.2 copy-start.8
  69.0 3.4 copy-start.4
  69.0 3.4 copy-start.12
  70.1 8.1 %copy-start.7 = (s32[1024]{0:T(1024)S(1)}, s32[1024]{0:T(1024)}, u32[]{:S(2)}) copy-start(s32[1024]{0:T(1024)} %pad_clamp_fusion.2) | copy-start | bytes 12292
  75.3 27.8 %collective-permute-start.1 = (bf16[16,67,256]{2,0,1:T(8,128)(2,1)}, bf16[16,67,256]{2,0,1:T(8,128)(2,1)}, u32[]{:S(2)}, u32[]{:S(2)}) collective-permute-start(bf16[16,67,256]{2,0,1:T(8,128)(2,1)} %bitcast.13), channel_id=1, source_target_pairs={{1,0},{2,1},{3,2},{4,3},{5,4},{6,5},{7,6},{8,7},{9,8},{10,9},{11,1... | collective-permute-start | bytes 1646600 | tf_op jit(solution)/shard_map/ppermute | solution.py:26
  78.3 4.6 %copy-start.11 = (pred[8,16]{1,0:T(8,128)(4,1)S(1)}, pred[8,16]{1,0:T(8,128)(4,1)}, u32[]{:S(2)}) copy-start(pred[8,16]{1,0:T(8,128)(4,1)} %get-tuple-element.157) | copy-start | bytes 388
  89.9 6.9 %copy-start.3 = (bf16[16,64,256]{2,1,0:T(8,128)(2,1)S(1)}, bf16[16,64,256]{2,1,0:T(8,128)(2,1)}, u32[]{:S(2)}) copy-start(bf16[16,64,256]{2,1,0:T(8,128)(2,1)} %param.25) | copy-start | bytes 1572868
  103.1 3.4 copy-start.13
  110.1 1.0 copy-start.1
  135.2 1.0 copy-start.1
  147.7 1.0 copy-start.1
  235.5 1.0 copy-start.1
  248.0 1.0 copy-start.1
  307.0 2.9 copy-start.2
  307.0 2.9 copy-start.6
  (11 other events, 10.5 us)
where the time goes:
time: 361 us; the launch traced here: 355 us
  matrix products  175 us (48%)
  local copies, waits for them, and re-layouts  90 us (25%)
  other arithmetic  51.3 us (14%)
  blocking collectives  18.8 us (5%)
  starting transfers between devices  18.7 us (5%)
    dot_general x16, matrix products, near_leaf(): jnp.einsum('nts,nps->pt', kernel_block, masked_values, preferred_element_...  105 us
    dot_general x8, matrix products, place_block(): jnp.dot(combined, selector, precision=lax.Precision.HIGHEST, preferred_el...  34.1 us
    gather x16, local copies, waits for them, and re-layouts, near_leaf(): sources = jnp.take(extended, neighbors - leaf_offset, axis=0)  33.4 us
    dot_general x8, matrix products, gather_block(): jnp.dot(stacked, selector, preferred_element_type=jnp.float32)  20.2 us
    all_gather x1, blocking collectives, per_device(): gathered = lax.all_gather(top_flat, 'col', axis=0, tiled=True)  18.8 us
    gather x6, local copies, waits for them, and re-layouts, apply_coupling(): sources = jnp.take(rows, positions, axis=0)  17.7 us
    while x64, local copies, waits for them, and re-layouts  15.4 us
    select_n x32, other arithmetic, near_leaf(): sources = jnp.take(extended, neighbors - leaf_offset, axis=0)  13.7 us
  transfers between devices with their start and end apart: 6, of which 0 were waited for; matrix products, arithmetic and copies ran while one was open for 10% of the time, Pallas kernels for 0%

commit v1 on v0

v1 whole, which is shorter than its diff:
```python
import jax
import jax.numpy as jnp
from jax import lax
from jax.experimental import pallas as pl
from jax.experimental.pallas import tpu as pltpu
from jax.sharding import PartitionSpec as P

LEAF = 256
AMPLITUDE = 0.125
LENGTH_SCALE = 1.0
GROUP = 4
FEATURES = 48
BF16 = jnp.bfloat16
F32 = jnp.float32
NT = (((1,), (1,)), ((), ()))


def dot(a, b):
    return jnp.dot(a, b, preferred_element_type=F32)


def dot_nt(a, b):
    return lax.dot_general(a, b, NT, preferred_element_type=F32)


def prep_kernel(
    order, near_count, coords, probes, near_list, basis, low, top,
    points_out, coef_out, counts_out, rows_in, rows_out,
):
    points = coords.shape[1]
    probe_rows = probes.shape[0]
    leaves = basis.shape[0]
    spans = lax.axis_size("col")
    device = lax.axis_index("col")

    for c in range(points // 256):
        at = slice(c * 256, c * 256 + 256)
        block = jnp.concatenate(
            [
                probes[:, at].astype(F32),
                coords[:, at].astype(F32),
                jnp.zeros((125 - probe_rows, 256), F32),
            ],
            axis=0,
        )
        rows_in[at, :] = block.T

    first = device * points

    @pl.loop(0, points // 16)
    def _(k):
        base = pl.multiple_of(k * 16, 16)
        for u in range(16):
            rows_out[pl.ds(base + u, 1), :] = rows_in[pl.ds(order[base + u] - first, 1), :]

    for c in range(points // 256):
        at = slice(c * 256, c * 256 + 256)
        points_out[:, at] = rows_out[at, :].T[:80, :].astype(BF16)

    lane = lax.broadcasted_iota(jnp.int32, (leaves, 128), 1)
    row = lax.broadcasted_iota(jnp.int32, (leaves, 128), 0)
    live = jnp.zeros((leaves, 128), jnp.int32)
    for i in range(leaves):
        live = jnp.where(row == i, near_count[i], live)
    start = device * leaves - leaves
    total = jnp.zeros((leaves, 128), jnp.int32)
    for k in range(near_list.shape[1]):
        named = near_list[:, k : k + 1] - start
        total = total + jnp.where((named == lane) & (live > k), 1, 0)
    inside = (lane + start >= 0) & (lane + start < spans * leaves)
    counts_out[...] = jnp.where(inside, total, 0)

    leaf_coef = [
        dot_nt(points_out[:probe_rows, i * LEAF : (i + 1) * LEAF], basis[i]).astype(BF16)
        for i in range(leaves)
    ]
    mid_coef = [
        (dot(leaf_coef[2 * m], low[2 * m]) + dot(leaf_coef[2 * m + 1], low[2 * m + 1])).astype(BF16)
        for m in range(leaves // 2)
    ]
    top_coef = [
        (dot(mid_coef[2 * q], top[2 * q]) + dot(mid_coef[2 * q + 1], top[2 * q + 1])).astype(BF16)
        for q in range(leaves // 4)
    ]
    nodes = leaf_coef + mid_coef + top_coef
    for m in range(len(nodes) // 2):
        coef_out[m] = jnp.concatenate([nodes[2 * m], nodes[2 * m + 1]], axis=1)


def target_features(cells):
    squares = cells * cells
    high = squares.astype(BF16).astype(F32)
    ones = jnp.ones_like(cells)
    return jnp.concatenate([cells, high, squares - high, ones, ones, jnp.zeros_like(cells)], axis=0)


def source_features(cells):
    squares = cells * cells
    high = squares.astype(BF16).astype(F32)
    ones = jnp.ones_like(cells)
    return jnp.concatenate(
        [-2.0 * cells, ones, ones, high, squares - high, jnp.zeros_like(cells)], axis=0
    )


def fill_targets(points, targets):
    for i in range(targets.shape[0]):
        cells = points[64:80, i * LEAF : (i + 1) * LEAF].astype(F32)[:8]
        targets[i] = target_features(cells).astype(BF16)


def fill_sources(points, sources, values, place):
    leaves = points.shape[1] // LEAF
    for i in range(leaves):
        cells = points[64:80, i * LEAF : (i + 1) * LEAF].astype(F32)[:8]
        sources[place + i] = source_features(cells).T.astype(BF16)
        values[place + i] = points[:64, i * LEAF : (i + 1) * LEAF]


def list_pairs(counts, listed, windows):
    leaves = counts.shape[0]
    position = jnp.int32(0)
    for i in range(leaves):
        for lane, slot in windows(i):
            count = counts[i, lane]
            listed[position] = count * 4096 + (i * 64 + slot)
            position = position + jnp.minimum(count, 1)
    for u in range(GROUP):
        listed[position + u] = jnp.int32(0)
    return (position + (GROUP - 1)) // GROUP


def add_pairs(listed, groups, targets, sources, values, field):
    @pl.loop(0, groups)
    def _(g):
        for u in range(GROUP):
            pair = listed[g * GROUP + u]
            slot = pair & 63
            leaf = (pair >> 6) & 63
            weight = (pair >> 12).astype(F32) * AMPLITUDE
            squared = jnp.maximum(dot(sources[slot], targets[leaf]), 1e-30)
            tile = jnp.exp(squared * lax.rsqrt(squared) * (-1.0 / LENGTH_SCALE)).astype(BF16)
            field[leaf] += dot(values[slot], tile) * weight


def own_kernel(counts, points, field, targets, sources, values, listed):
    leaves = targets.shape[0]
    fill_targets(points, targets)
    fill_sources(points, sources, values, 0)
    field[...] = jnp.zeros_like(field)
    groups = list_pairs(counts, listed, lambda i: [(leaves + j, j) for j in range(leaves)])
    add_pairs(listed, groups, targets, sources, values, field)


def rest_kernel(
    counts, order, far_leaf, far_mid, far_top,
    own, left, right, field_in, coef_own, coef_left, coef_right, tops,
    basis, low, top, couple_leaf_hbm, couple_mid_hbm, couple_top_hbm,
    out,
    targets, sources, values, listed, field,
    around_leaf, around_mid, around_top, couple_leaf, couple_mid, couple_top,
    couple_sum, rows_in, rows_out, sems,
):
    leaves = basis.shape[0]
    points = own.shape[1]
    device = lax.axis_index("col")
    copies = [
        pltpu.make_async_copy(couple_top_hbm, couple_top, sems.at[0]),
        pltpu.make_async_copy(couple_mid_hbm, couple_mid, sems.at[1]),
        pltpu.make_async_copy(couple_leaf_hbm, couple_leaf, sems.at[2]),
    ]
    for copy in copies:
        copy.start()

    fill_targets(own, targets)
    fill_sources(left, sources, values, 0)
    fill_sources(right, sources, values, leaves)
    field[...] = field_in[...]
    groups = list_pairs(
        counts,
        listed,
        lambda i: [(j, j) for j in range(i, leaves)]
        + [(2 * leaves + j, leaves + j) for j in range(i + 1)],
    )
    add_pairs(listed, groups, targets, sources, values, field)

    def spread(pair, around, slot):
        one, two = pair[:, :64], pair[:, 64:]
        around[slot] = jnp.concatenate([one, one], axis=1)
        around[slot + 1] = jnp.concatenate([two, two], axis=1)

    mids = leaves // 2
    for part, coefs in enumerate((coef_left, coef_own, coef_right)):
        for m in range(leaves // 2):
            spread(coefs[m], around_leaf, part * leaves + 2 * m)
        for m in range(mids // 2):
            spread(coefs[leaves // 2 + m], around_mid, part * mids + 2 * m)

    @pl.loop(0, tops.shape[0])
    def _(m):
        spread(tops[m], around_top, 2 * m)

    for copy in copies:
        copy.wait()

    lower_half = lax.broadcasted_iota(jnp.int32, (64, 128), 1) < 64

    def couple(lists, around, matrices, base, place):
        far = lists.shape[1]

        @pl.loop(0, lists.shape[0])
        def _(n):
            total = jnp.zeros((64, 64), F32)
            for f in range(0, far, 4):
                picked = [around[lists[n, f + d] - base] for d in range(4)]
                rows = jnp.concatenate(
                    [
                        jnp.where(lower_half, picked[0], picked[1]),
                        jnp.where(lower_half, picked[2], picked[3]),
                    ],
                    axis=1,
                )
                total = total + dot(rows, matrices[n, f : f + 4].reshape(256, 64))
            couple_sum[place + n] = total

    couple(far_top, around_top, couple_top, 0, leaves + mids)
    couple(far_mid, around_mid, couple_mid, device * mids - mids, leaves)
    couple(far_leaf, around_leaf, couple_leaf, device * leaves - leaves, 0)

    for m in range(mids):
        parent = couple_sum[leaves + mids + m // 2].astype(BF16)
        couple_sum[leaves + m] += dot_nt(parent, top[m])
    for i in range(leaves):
        parent = couple_sum[leaves + i // 2].astype(BF16)
        couple_sum[i] += dot_nt(parent, low[i])
    for i in range(leaves):
        total = field[i] + dot(couple_sum[i].astype(BF16), basis[i])
        rows_in[i * LEAF : (i + 1) * LEAF, :] = jnp.concatenate(
            [total, jnp.zeros_like(total)], axis=0
        ).T

    first = device * points

    @pl.loop(0, points // 16)
    def _(k):
        base = pl.multiple_of(k * 16, 16)
        for u in range(16):
            rows_out[pl.ds(order[base + u] - first, 1), :] = rows_in[pl.ds(base + u, 1), :]

    for c in range(points // 256):
        at = slice(c * 256, c * 256 + 256)
        out[:, at] = rows_out[at, :].T[:64, :]


def vmem():
    return pl.BlockSpec(memory_space=pltpu.VMEM)


def smem():
    return pl.BlockSpec(memory_space=pltpu.SMEM)


def params():
    return pltpu.CompilerParams(vmem_limit_bytes=50 * 2**20)


def per_device(
    coords, probes, order, near_list, near_count, leaf_basis, transfer_low, transfer_top,
    coupling_leaf, coupling_mid, coupling_top, far_leaf, far_mid, far_top,
):
    points = coords.shape[1]
    leaves = leaf_basis.shape[0]
    mids, tops = leaves // 2, leaves // 4
    count = lax.axis_size("col")
    shape = jax.ShapeDtypeStruct

    tree, coef, counts = pl.pallas_call(
        prep_kernel,
        out_shape=(
            shape((80, points), BF16),
            shape(((leaves + mids + tops) // 2, 64, 128), BF16),
            shape((leaves, 128), jnp.int32),
        ),
        in_specs=[smem(), smem()] + [vmem()] * 6,
        out_specs=(vmem(), vmem(), vmem()),
        scratch_shapes=[pltpu.VMEM((points, 128), F32)] * 2,
        compiler_params=params(),
        cost_estimate=pl.CostEstimate(flops=10**9, bytes_accessed=2 * 10**7, transcendentals=0),
        name="prep",
    )(order, near_count, coords, probes, near_list, leaf_basis, transfer_low, transfer_top)

    ahead = [(i, i + 1) for i in range(count - 1)]
    back = [(i + 1, i) for i in range(count - 1)]
    shared = coef[: (leaves + mids) // 2]
    left = lax.ppermute(tree, "col", ahead)
    right = lax.ppermute(tree, "col", back)
    coef_left = lax.ppermute(shared, "col", ahead)
    coef_right = lax.ppermute(shared, "col", back)
    gathered = lax.all_gather(coef[(leaves + mids) // 2 :], "col", axis=0, tiled=True)

    field = pl.pallas_call(
        own_kernel,
        out_shape=shape((leaves, 64, LEAF), F32),
        in_specs=[smem(), vmem()],
        out_specs=vmem(),
        scratch_shapes=[
            pltpu.VMEM((leaves, FEATURES, LEAF), BF16),
            pltpu.VMEM((leaves, LEAF, FEATURES), BF16),
            pltpu.VMEM((leaves, 64, LEAF), BF16),
            pltpu.SMEM((leaves * leaves + GROUP,), jnp.int32),
        ],
        compiler_params=params(),
        cost_estimate=pl.CostEstimate(
            flops=2 * 10**10, bytes_accessed=2 * 10**7, transcendentals=10**7
        ),
        name="own_pairs",
    )(counts, tree)

    return pl.pallas_call(
        rest_kernel,
        out_shape=shape((64, points), F32),
        in_specs=[smem()] * 5 + [vmem()] * 11 + [pl.BlockSpec(memory_space=pl.ANY)] * 3,
        out_specs=vmem(),
        scratch_shapes=[
            pltpu.VMEM((leaves, FEATURES, LEAF), BF16),
            pltpu.VMEM((2 * leaves, LEAF, FEATURES), BF16),
            pltpu.VMEM((2 * leaves, 64, LEAF), BF16),
            pltpu.SMEM((leaves * (leaves + 1) + GROUP,), jnp.int32),
            pltpu.VMEM((leaves, 64, LEAF), F32),
            pltpu.VMEM((3 * leaves, 64, 128), BF16),
            pltpu.VMEM((3 * mids, 64, 128), BF16),
            pltpu.VMEM((tops * count, 64, 128), BF16),
            pltpu.VMEM(coupling_leaf.shape, BF16),
            pltpu.VMEM(coupling_mid.shape, BF16),
            pltpu.VMEM(coupling_top.shape, BF16),
            pltpu.VMEM((leaves + mids + tops, 64, 64), F32),
            pltpu.VMEM((points, 128), F32),
            pltpu.VMEM((points, 128), F32),
            pltpu.SemaphoreType.DMA((3,)),
        ],
        compiler_params=params(),
        cost_estimate=pl.CostEstimate(
            flops=2 * 10**10, bytes_accessed=2 * 10**7, transcendentals=10**7
        ),
        name="rest",
    )(
        counts, order, far_leaf, far_mid, far_top,
        tree, left, right, field, coef, coef_left, coef_right, gathered,
        leaf_basis, transfer_low, transfer_top, coupling_leaf, coupling_mid, coupling_top,
    )


def solution(mesh):
    both = ("groups", "col")
    return jax.shard_map(
        per_device,
        mesh=mesh,
        in_specs=(
            P(None, both),
            P(None, both),
            P(both),
            P(both, None),
            P(both),
            P(both, None, None),
            P(both, None, None),
            P(both, None, None),
            P(both, None, None, None),
            P(both, None, None, None),
            P(both, None, None, None),
            P(both, None),
            P(both, None),
            P(both, None),
        ),
        out_specs=P(None, both),
        check_vma=False,
    )
```

time: 361 us -> 120 us (0.33); the launches traced: 355 us -> 120 us
  matrix products: 175 us -> 0 us
  local copies, waits for them, and re-layouts: 90 us -> 7.8 us
  Pallas kernels: 0 us -> 77.8 us
  other arithmetic: 51.3 us -> 0 us
  starting transfers between devices: 18.7 us -> 12.9 us
    dot_general x38 -> x0, matrix products: 175 us -> none  [the longest x16 105 us: near_leaf(): jnp.einsum('nts,nps->pt', kernel_block, masked_values, preferred_element_...]
    pallas_call x0 -> x3, Pallas kernels: none -> 77.8 us  [the longest x1 43.9 us: per_device(): pl.pallas_call(rest_kernel, out_shape=shape((64, points), F32), in_specs=...]
    gather x22 -> x0, local copies, waits for them, and re-layouts: 51.1 us -> none  [the longest x16 33.4 us: near_leaf(): sources = jnp.take(extended, neighbors - leaf_offset, axis=0)]
    while x66 -> x0, local copies, waits for them, and re-layouts: 17.2 us -> none
    dynamic_slice x32 -> x0, local copies, waits for them, and re-layouts: 14.5 us -> none  [the longest x16 9.78 us: per_device(): near_blocks = lax.map(near_leaf, (near_list, near_count, leaf_major[:, :3]))]
    select_n x33 -> x0, other arithmetic: 13.7 us -> none  [the longest x32 13.7 us: near_leaf(): sources = jnp.take(extended, neighbors - leaf_offset, axis=0)]
    and x19 -> x0, other arithmetic: 12.4 us -> none  [the longest x16 11.3 us: near_leaf(): sources = jnp.take(extended, neighbors - leaf_offset, axis=0)]
    convert_element_type x32 -> x0, other arithmetic: 10.4 us -> none  [the longest x16 10.2 us: near_leaf(): (jnp.arange(NEAR, dtype=jnp.int32) < live_count).astype(jnp.bfloat16)]
  transfers between devices with their start and end apart: 6 -> 4, of which waited for: 0 -> 0; matrix products, arithmetic and copies ran while one was open for 10% -> 0% of each run, Pallas kernels for 0% -> 22%
where the time goes in v1:
time: 120 us
  Pallas kernels  77.8 us (65%)
  blocking collectives  21.1 us (18%)
  starting transfers between devices  12.9 us (11%)
  local copies, waits for them, and re-layouts  7.8 us (6%)
    pallas_call x1, Pallas kernels, per_device(): pl.pallas_call(rest_kernel, out_shape=shape((64, points), F32), in_specs=...  43.9 us
    pallas_call x1, Pallas kernels, per_device(): pl.pallas_call(own_kernel, out_shape=shape((leaves, 64, LEAF), F32), in_s...  26.2 us
    all_gather x1, blocking collectives, per_device(): lax.all_gather(coef[(leaves + mids) // 2:], 'col', axis=0, tiled=True)  21.1 us
    unnamed x30, local copies, waits for them, and re-layouts  7.77 us
    pallas_call x1, Pallas kernels, per_device(): pl.pallas_call(prep_kernel, out_shape=(shape((80, points), BF16), shape((...  7.64 us
    ppermute x1, starting transfers between devices, per_device(): left = lax.ppermute(tree, 'col', ahead)  4.54 us
    ppermute x1, starting transfers between devices, per_device(): coef_left = lax.ppermute(shared, 'col', ahead)  3.88 us
    ppermute x1, starting transfers between devices, per_device(): coef_right = lax.ppermute(shared, 'col', back)  2.58 us
  transfers between devices with their start and end apart: 4, of which 0 were waited for; matrix products, arithmetic and copies ran while one was open for 0% of the time, Pallas kernels for 22%

profile of v1, /device:TPU:5, one launch (start us, length us, event | category | flops | bytes accessed | tf_op | source)
XLA Modules:
  0.0 119.7 jit_solution(577215278941423565)
XLA Ops:
  0.0 1.0 copy-done
  1.0 1.0 copy-done.1
  2.1 0.9 copy-done.3
  3.0 0.9 copy-done.5
  3.9 0.8 copy-done.7
  4.7 0.7 copy-done.8
  5.4 0.7 copy-done.9
  6.1 0.7 copy-done.13
  6.8 7.6 %prep.1 = (bf16[80,4096]{1,0:T(8,128)(2,1)S(1)}, bf16[14,64,128]{2,1,0:T(8,128)(2,1)S(1)}, s32[16,128]{1,0:T(8,128)S(1)}) custom-call(s32[4096]{0:T(1024)S(1)} %copy-done.8, s32[16]{0:T(128)S(1)} %copy-done.13, bf16[3,4096]{1,0:T(4,128)(2,1)S(1)} %copy-done.7, bf16[64,4096]{1,0:T(8,128)(2,1)S(1)} %copy-done, s32[16,27]{1,0:T(8,128)S(1)} %copy-done.9, ...), custom_call_target="tpu_custom_call" | custom-call | flops 1000000000 | bytes 20000000 | tf_op jit(solution)/shard_map/prep/pallas_call | solution.py:277
  14.4 2.6 %collective-permute-start.3 = (bf16[12,64,128]{2,1,0:T(8,128)(2,1)S(1)}, bf16[12,64,128]{2,1,0:T(8,128)(2,1)S(1)}, u32[]{:S(2)}, u32[]{:S(2)}) collective-permute-start(bf16[12,64,128]{2,1,0:T(8,128)(2,1)S(1)} %slice.6), channel_id=1, source_target_pairs={{1,0},{2,1},{3,2},{4,3},{5,4},{6,5},{7,6},{8,7},{9,8},{10,9},{11,1... | collective-permute-start | bytes 589832 | tf_op jit(solution)/shard_map/ppermute | solution.py:298
  17.0 3.9 %collective-permute-start.2 = (bf16[12,64,128]{2,1,0:T(8,128)(2,1)S(1)}, bf16[12,64,128]{2,1,0:T(8,128)(2,1)S(1)}, u32[]{:S(2)}, u32[]{:S(2)}) collective-permute-start(bf16[12,64,128]{2,1,0:T(8,128)(2,1)S(1)} %slice.6), channel_id=1, source_target_pairs={{0,1},{1,2},{2,3},{3,4},{4,5},{5,6},{6,7},{7,8},{8,9},{9,10},{10,1... | collective-permute-start | bytes 589832 | tf_op jit(solution)/shard_map/ppermute | solution.py:297
  20.9 1.9 %collective-permute-start.1 = (bf16[80,4096]{1,0:T(8,128)(2,1)S(1)}, bf16[80,4096]{1,0:T(8,128)(2,1)S(1)}, u32[]{:S(2)}, u32[]{:S(2)}) collective-permute-start(bf16[80,4096]{1,0:T(8,128)(2,1)S(1)} %get-tuple-element.9.points.own), channel_id=1, source_target_pairs={{1,0},{2,1},{3,2},{4,3},{5,4},{6,5},{7,6},{8,7},{9,8},{10,9},{11,1... | collective-permute-start | bytes 1966088 | tf_op jit(solution)/shard_map/ppermute | solution.py:296
  22.8 4.5 %collective-permute-start = (bf16[80,4096]{1,0:T(8,128)(2,1)S(1)}, bf16[80,4096]{1,0:T(8,128)(2,1)S(1)}, u32[]{:S(2)}, u32[]{:S(2)}) collective-permute-start(bf16[80,4096]{1,0:T(8,128)(2,1)S(1)} %get-tuple-element.9.points.own), channel_id=1, source_target_pairs={{0,1},{1,2},{2,3},{3,4},{4,5},{5,6},{6,7},{7,8},{8,9},{9,10},{10,1... | collective-permute-start | bytes 1966088 | tf_op jit(solution)/shard_map/ppermute | solution.py:295
  27.4 0.0 copy-start.2
  27.4 0.0 copy-start.4
  27.4 0.0 copy-start.6
  27.4 0.0 copy-start.10
  27.4 0.0 copy-start.11
  27.5 0.0 copy-start.12
  27.5 26.2 %own_pairs.1.field_in = f32[16,64,256]{2,1,0:T(8,128)S(1)} custom-call(s32[16,128]{1,0:T(8,128)S(1)} %get-tuple-element.8.counts, bf16[80,4096]{1,0:T(8,128)(2,1)S(1)} %get-tuple-element.9.points.own), custom_call_target="tpu_custom_call" | custom-call | flops 20000000000 | bytes 20000000 | tf_op jit(solution)/shard_map/own_pairs/pallas_call | solution.py:301
  53.7 1.0 copy-done.14
  54.7 21.1 %all_gather.3.tops = bf16[32,64,128]{2,1,0:T(8,128)(2,1)S(1)} all-gather(bf16[2,64,128]{2,1,0:T(8,128)(2,1)S(1)} %slice.7), channel_id=1, replica_groups=mesh['groups'=2,'col'=16] {'col'}, dimensions={0}, use_global_device_ids=true | all-gather | bytes 557056 | tf_op jit(solution)/shard_map/all_gather | solution.py:299
  75.7 0.0 collective-permute-done.3.coef_right
  75.8 43.9 %rest.1 = f32[64,4096]{1,0:T(8,128)} custom-call(s32[16,128]{1,0:T(8,128)S(1)} %get-tuple-element.8.counts, s32[4096]{0:T(1024)S(1)} %copy-done.8, s32[16,16]{1,0:T(8,128)S(1)} %copy-done.10, s32[8,16]{1,0:T(8,128)S(1)} %copy-done.11, s32[4,16]{1,0:T(4,128)S(1)} %copy-done.12, bf16[80,4096]{1,0:T(8,128)(2,1)S(1)} %get-tuple-element.9.points.own, ...), custom_call_target="tpu_custom_call" | custom-call | flops 20000000000 | bytes 20000000 | tf_op jit(solution)/shard_map/rest/pallas_call | solution.py:319
  (20 shorter events, 0.1 us)
Async XLA Ops:
  0.0 1.0 copy-start
  1.0 1.0 copy-start.1
  2.1 0.9 copy-start.3
  3.0 0.9 copy-start.5
  3.9 0.8 copy-start.7
  4.7 0.7 copy-start.8
  5.4 0.7 copy-start.9
  6.1 0.7 copy-start.13
  14.4 61.3 %collective-permute-start.3 = (bf16[12,64,128]{2,1,0:T(8,128)(2,1)S(1)}, bf16[12,64,128]{2,1,0:T(8,128)(2,1)S(1)}, u32[]{:S(2)}, u32[]{:S(2)}) collective-permute-start(bf16[12,64,128]{2,1,0:T(8,128)(2,1)S(1)} %slice.6), channel_id=1, source_target_pairs={{1,0},{2,1},{3,2},{4,3},{5,4},{6,5},{7,6},{8,7},{9,8},{10,9},{11,1... | collective-permute-start | bytes 589832 | tf_op jit(solution)/shard_map/ppermute | solution.py:298
  17.0 58.7 %collective-permute-start.2 = (bf16[12,64,128]{2,1,0:T(8,128)(2,1)S(1)}, bf16[12,64,128]{2,1,0:T(8,128)(2,1)S(1)}, u32[]{:S(2)}, u32[]{:S(2)}) collective-permute-start(bf16[12,64,128]{2,1,0:T(8,128)(2,1)S(1)} %slice.6), channel_id=1, source_target_pairs={{0,1},{1,2},{2,3},{3,4},{4,5},{5,6},{6,7},{7,8},{8,9},{9,10},{10,1... | collective-permute-start | bytes 589832 | tf_op jit(solution)/shard_map/ppermute | solution.py:297
  20.9 54.8 %collective-permute-start.1 = (bf16[80,4096]{1,0:T(8,128)(2,1)S(1)}, bf16[80,4096]{1,0:T(8,128)(2,1)S(1)}, u32[]{:S(2)}, u32[]{:S(2)}) collective-permute-start(bf16[80,4096]{1,0:T(8,128)(2,1)S(1)} %get-tuple-element.9.points.own), channel_id=1, source_target_pairs={{1,0},{2,1},{3,2},{4,3},{5,4},{6,5},{7,6},{8,7},{9,8},{10,9},{11,1... | collective-permute-start | bytes 1966088 | tf_op jit(solution)/shard_map/ppermute | solution.py:296
  22.8 52.9 %collective-permute-start = (bf16[80,4096]{1,0:T(8,128)(2,1)S(1)}, bf16[80,4096]{1,0:T(8,128)(2,1)S(1)}, u32[]{:S(2)}, u32[]{:S(2)}) collective-permute-start(bf16[80,4096]{1,0:T(8,128)(2,1)S(1)} %get-tuple-element.9.points.own), channel_id=1, source_target_pairs={{0,1},{1,2},{2,3},{3,4},{4,5},{5,6},{6,7},{7,8},{8,9},{9,10},{10,1... | collective-permute-start | bytes 1966088 | tf_op jit(solution)/shard_map/ppermute | solution.py:295
  27.4 48.4 %copy-start.2 = (bf16[16,64,256]{2,1,0:T(8,128)(2,1)S(1)}, bf16[16,64,256]{2,1,0:T(8,128)(2,1)}, u32[]{:S(2)}) copy-start(bf16[16,64,256]{2,1,0:T(8,128)(2,1)} %basis.3) | copy-start | bytes 1572868
  27.4 48.4 %copy-start.4 = (bf16[16,64,64]{2,1,0:T(8,128)(2,1)S(1)}, bf16[16,64,64]{2,1,0:T(8,128)(2,1)}, u32[]{:S(2)}) copy-start(bf16[16,64,64]{2,1,0:T(8,128)(2,1)} %low.3) | copy-start | bytes 393220
  27.4 48.4 %copy-start.6 = (bf16[8,64,64]{2,1,0:T(8,128)(2,1)S(1)}, bf16[8,64,64]{2,1,0:T(8,128)(2,1)}, u32[]{:S(2)}) copy-start(bf16[8,64,64]{2,1,0:T(8,128)(2,1)} %top.3) | copy-start | bytes 196612
  27.4 48.4 %copy-start.10 = (s32[16,16]{1,0:T(8,128)S(1)}, s32[16,16]{1,0:T(8,128)}, u32[]{:S(2)}) copy-start(s32[16,16]{1,0:T(8,128)} %far_leaf.1) | copy-start | bytes 3076
  27.4 48.4 %copy-start.11 = (s32[8,16]{1,0:T(8,128)S(1)}, s32[8,16]{1,0:T(8,128)}, u32[]{:S(2)}) copy-start(s32[8,16]{1,0:T(8,128)} %far_mid.1) | copy-start | bytes 1540
  27.5 48.4 %copy-start.12 = (s32[4,16]{1,0:T(4,128)S(1)}, s32[4,16]{1,0:T(4,128)}, u32[]{:S(2)}) copy-start(s32[4,16]{1,0:T(4,128)} %far_top.1) | copy-start | bytes 772
  53.7 1.0 copy-start.14
